TPU v7x, 32 devices: a whole 2x2x4 slice. The times are simulated.
32 devices in a mesh: gx: 4 (over y, core), gy: 4 (over z), gz: 2 (over x).
Axes of the slice: x: 2, y: 2, z: 4, core: 2. Of those that a mesh axis runs over, the one named last changes fastest.
Arguments:
- tokens: bfloat16 [1024, 8192], P(('gx', 'gy'), 'gz'), may hold values from -6 to 6
- gate_weight: bfloat16 [8192, 28672], P('gz', ('gx', 'gy')), may hold values from -0.0625 to 0.0625
- up_weight: bfloat16 [8192, 28672], P('gz', ('gx', 'gy')), may hold values from -0.0625 to 0.0625
- down_weight: bfloat16 [28672, 8192], P(('gx', 'gy'), 'gz'), may hold values from -0.03125 to 0.03125
Outputs:
- layer_output: bfloat16 [1024, 8192], P(('gx', 'gy'), 'gz')
All inputs are finite; a program needn't handle non-finite values.
Results may differ from a plain program's by a relative error of at most 0.029.
Values may be sent and summed in bfloat16 or wider, within the bound.
No kernel may reach another device: no remote copies, remote signals or barrier semaphores. Data moves between devices by JAX's collectives and lax.ppermute only.
A program may use at most 256 MiB of HBM per device.

v0:
```python
import jax
import jax.numpy as jnp
from jax import lax
from jax.sharding import PartitionSpec as P


def shards(tokens, gate_weight, up_weight, down_weight):
    gathered = lax.all_gather(tokens, "gx", axis=0, tiled=True)

    def column_product(weight_piece):
        return jnp.dot(gathered, weight_piece, preferred_element_type=jnp.float32)

    gate_partial = column_product(lax.all_gather(gate_weight, "gy", axis=1, tiled=True))
    up_partial = column_product(lax.all_gather(up_weight, "gy", axis=1, tiled=True))
    gate_sum, up_sum = (
        lax.psum_scatter(
            gate_partial.astype(jnp.bfloat16), "gz", scatter_dimension=0, tiled=True
        ).astype(jnp.float32),
        lax.psum_scatter(
            up_partial.astype(jnp.bfloat16), "gz", scatter_dimension=0, tiled=True
        ).astype(jnp.float32),
    )
    local_hidden = (jax.nn.silu(gate_sum) * up_sum).astype(jnp.bfloat16)
    hidden = lax.all_gather(local_hidden, "gz", axis=0, tiled=True)
    down_partial = jnp.dot(
        hidden,
        lax.all_gather(down_weight, "gy", axis=0, tiled=True),
        preferred_element_type=jnp.float32,
    )
    layer_output = lax.psum_scatter(
        down_partial.astype(jnp.bfloat16), "gx", scatter_dimension=0, tiled=True
    )
    return layer_output


def solution(mesh):
    return jax.shard_map(
        shards,
        mesh=mesh,
        in_specs=(
            P(("gx", "gy"), "gz"),
            P("gz", ("gx", "gy")),
            P("gz", ("gx", "gy")),
            P(("gx", "gy"), "gz"),
        ),
        out_specs=P(("gx", "gy"), "gz"),
        check_vma=False,
    )
```

profile of v0, /device:TPU:0, one launch (start us, length us, event | category | flops | bytes accessed | tf_op | source)
XLA Modules:
  0.0 3175.0 jit_solution(5421963953464230407)
XLA Ops:
  6.5 0.0 all-gather.6.cloned.1.call-start
  6.5 0.7 all-gather.6.cloned.1.call-update
  7.3 0.0 all-gather.8.cloned.1.call-start
  7.3 0.7 all-gather.8.cloned.1.call-update
  8.0 0.0 all-gather.10.cloned.1.call-start
  8.1 0.7 all-gather.10.cloned.1.call-update
  8.7 0.0 reduce-scatter.4.cloned.1.call-start
  8.8 25.5 all-gather.6.cloned.1.call-done
  34.2 976.0 %all-gather.8.cloned.1.call-done = bf16[4096,7168]{1,0:T(8,128)(2,1)} async-done(((bf16[4096,1792]{1,0:T(8,128)(2,1)}), bf16[4096,7168]{1,0:T(8,128)(2,1)}) %all-gather.8.cloned.1.call-update) | async-done | bytes 58720272 | tf_op jit(solution)/shard_map/all_gather | solution.py:13
  1010.2 36.2 %convolution_convert_fusion.1 = bf16[256,7168]{1,0:T(8,128)(2,1)} fusion(bf16[256,4096]{1,0:T(8,128)(2,1)} %all-gather.6.cloned.1.call-done, bf16[4096,7168]{1,0:T(8,128)(2,1)} %all-gather.8.cloned.1.call-done), kind=kOutput, calls=%fused_computation.1 | convolution fusion | flops 15034220544 | bytes 64487424 | tf_op jit(solution)/shard_map/dot_general | solution.py:11
  1046.4 0.0 copy-start
  1046.4 0.0 reduce-scatter.4.cloned.1.call-update
  1046.5 0.0 reduce-scatter.6.cloned.1.call-start
  1046.5 937.9 %all-gather.10.cloned.1.call-done = bf16[4096,7168]{1,0:T(8,128)(2,1)} async-done(((bf16[4096,1792]{1,0:T(8,128)(2,1)}), bf16[4096,7168]{1,0:T(8,128)(2,1)}) %all-gather.10.cloned.1.call-update) | async-done | bytes 58720272 | tf_op jit(solution)/shard_map/all_gather | solution.py:14
  1984.4 0.0 copy-done
  1984.4 26.1 convolution_convert_fusion
  2010.5 0.0 reduce-scatter.6.cloned.1.call-update
  2010.5 0.0 all-gather.14.cloned.1.call-start
  2010.6 0.5 all-gather.14.cloned.1.call-update
  2011.1 0.0 all-gather.12.cloned.1.call-start
  2011.2 22.7 reduce-scatter.4.cloned.1.call-done
  2033.8 51.3 %reduce-scatter.6.cloned.1.call-done = bf16[128,7168]{1,0:T(8,128)(2,1)} async-done(((bf16[256,7168]{1,0:T(8,128)(2,1)}), bf16[128,7168]{1,0:T(8,128)(2,1)}) %reduce-scatter.6.cloned.1.call-update) | async-done | bytes 1835024 | tf_op jit(solution)/shard_map/reduce_scatter | solution.py:19
  2085.2 4.4 fusion.4
  2089.6 0.0 all-gather.12.cloned.1.call-update
  2089.6 0.2 reduce-scatter.8.cloned.1.call-start
  2089.8 971.2 %all-gather.14.cloned.1.call-done = bf16[7168,4096]{1,0:T(8,128)(2,1)} async-done(((bf16[1792,4096]{1,0:T(8,128)(2,1)}), bf16[7168,4096]{1,0:T(8,128)(2,1)}) %all-gather.14.cloned.1.call-update) | async-done | bytes 58720272 | tf_op jit(solution)/shard_map/all_gather | solution.py:27
  3061.1 50.6 %all-gather.12.cloned.1.call-done = bf16[256,7168]{1,0:T(8,128)(2,1)} async-done(((bf16[128,7168]{1,0:T(8,128)(2,1)}), bf16[256,7168]{1,0:T(8,128)(2,1)}) %all-gather.12.cloned.1.call-update) | async-done | bytes 3670032 | tf_op jit(solution)/shard_map/all_gather | solution.py:24
  3111.7 24.9 convolution_convert_fusion.2
  3136.6 0.0 reduce-scatter.8.cloned.1.call-update
  3136.6 31.6 reduce-scatter.8.cloned.1.call-done
Async XLA Ops:
  6.5 27.7 all-gather.6.cloned.1.call-start
  7.3 1003.0 %all-gather.8.cloned.1.call-start = ((), (), s32[]{:S(2)}) async-start(), calls=%async_computation.4 | async-start | bytes 73400320 | tf_op jit(solution)/shard_map/all_gather | solution.py:13
  8.0 1976.4 %all-gather.10.cloned.1.call-start = ((), (), s32[]{:S(2)}) async-start(), calls=%async_computation.6 | async-start | bytes 73400320 | tf_op jit(solution)/shard_map/all_gather | solution.py:14
  8.7 2025.1 %reduce-scatter.4.cloned.1.call-start = ((), (), s32[]{:S(2)}) async-start(), calls=%async_computation.5 | async-start | bytes 5505024 | tf_op jit(solution)/shard_map/reduce_scatter | solution.py:16
  1046.4 938.0 %copy-start = (bf16[256,4096]{1,0:T(8,128)(2,1)S(1)}, bf16[256,4096]{1,0:T(8,128)(2,1)}, u32[]{:S(2)}) copy-start(bf16[256,4096]{1,0:T(8,128)(2,1)} %all-gather.6.cloned.1.call-done) | copy-start | bytes 6291460
  1046.5 1038.7 %reduce-scatter.6.cloned.1.call-start = ((), (), s32[]{:S(2)}) async-start(), calls=%async_computation.7 | async-start | bytes 5505024 | tf_op jit(solution)/shard_map/reduce_scatter | solution.py:19
  2010.5 1050.5 %all-gather.14.cloned.1.call-start = ((), (), s32[]{:S(2)}) async-start(), calls=%async_computation.9 | async-start | bytes 73400320 | tf_op jit(solution)/shard_map/all_gather | solution.py:27
  2011.1 1100.5 %all-gather.12.cloned.1.call-start = ((), (), s32[]{:S(2)}) async-start(), calls=%async_computation.8 | async-start | bytes 5505024 | tf_op jit(solution)/shard_map/all_gather | solution.py:24
  2089.6 1078.6 %reduce-scatter.8.cloned.1.call-start = ((), (), s32[]{:S(2)}) async-start(), calls=%async_computation.10 | async-start | bytes 2621440 | tf_op jit(solution)/shard_map/reduce_scatter | solution.py:30
Sparse Core Ops, SparseCore 0:
  8.9 25.2 all-gather.5
  35.8 974.3 all-gather.7
  1011.8 972.5 all-gather.9
  1986.5 47.2 reduce-scatter.3
  2036.0 49.0 reduce-scatter.5
  2086.6 974.4 all-gather.13
  3062.6 49.0 all-gather.11
  3136.7 31.4 reduce-scatter.7
where the time goes:
time: 3180 us
  waiting for transfers between devices  3070 us (97%)
  matrix products  87.2 us (3%)
    all_gather x1, waiting for transfers between devices, shards(): lax.all_gather(gate_weight, 'gy', axis=1, tiled=True)  976 us
    all_gather x1, waiting for transfers between devices, shards(): lax.all_gather(down_weight, 'gy', axis=0, tiled=True)  971 us
    all_gather x1, waiting for transfers between devices, shards(): lax.all_gather(up_weight, 'gy', axis=1, tiled=True)  938 us
  transfers between devices with their start and end apart: 8, of which 8 were waited for; matrix products, arithmetic and copies ran while one was open for 2% of the time, Pallas kernels for 0%

commit v1 on v0

v1 whole, which is shorter than its diff:
```python
import functools

import jax
import jax.numpy as jnp
from jax import lax
from jax.experimental import pallas as pl
from jax.experimental.pallas import tpu as pltpu
from jax.sharding import PartitionSpec as P

BF16 = jnp.bfloat16
F32 = jnp.float32
MIB = 1 << 20


def tile_of(width, most):
    return max(t for t in range(128, most + 1, 128) if width % t == 0)


def in_vmem(array):
    return pltpu.with_memory_space_constraint(array, pltpu.VMEM)


def gate_up(position, blocks, gate, up, loads, n, load_gate_up):
    rows, depth = blocks[0].shape
    width = gate.shape[1]
    nb, part = len(blocks), rows // n
    tile = tile_of(width, 256)
    tiles = width // tile
    kept = [gate, up] * load_gate_up + list(loads)

    def body(*refs):
        refs = list(refs)
        take = lambda count: [refs.pop(0) for _ in range(count)]
        (where,), tokens, (gate_in, up_in), load_in = take(1), take(nb), take(2), take(len(loads))
        sums, kept_out = take(n), take(len(kept))
        left, product, block_sem, tile_sem, load_sem = refs
        copies = [
            pltpu.make_async_copy(tokens[b], left.at[pl.ds(b * rows, rows)], block_sem.at[b]) for b in range(nb)
        ]
        for copy in copies:
            copy.start()
        if load_gate_up:
            weights = kept_out[:2]

            def tile_copies(t):
                columns = pl.ds(pl.multiple_of(t * tile, tile), tile)
                return [
                    pltpu.make_async_copy(source.at[:, columns], target.at[:, columns], tile_sem.at[t, k])
                    for k, (source, target) in enumerate(zip((gate_in, up_in), weights))
                ]

            def start(t, carry):
                for copy in tile_copies(t):
                    copy.start()
                return carry

            lax.fori_loop(0, tiles, start, 0)
        else:
            weights = (gate_in, up_in)
        load_copies = [
            pltpu.make_async_copy(source, target, load_sem.at[k])
            for k, (source, target) in enumerate(zip(load_in, kept_out[len(kept) - len(loads):]))
        ]
        for copy in load_copies:
            copy.start()
        for copy in copies:
            copy.wait()
        position = where[0]

        def step(t, carry):
            columns = pl.ds(pl.multiple_of(t * tile, tile), tile)
            if load_gate_up:
                for copy in tile_copies(t):
                    copy.wait()
            for k in range(2):
                product[...] = jnp.dot(left[...], weights[k][:, columns], preferred_element_type=F32)
                for j in range(n):
                    at = lax.rem(position + j, n) * part
                    parts = [
                        product[pl.ds(pl.multiple_of(b * rows + at, part), part), :] for b in range(nb)
                    ]
                    sums[j][k, :, columns] = jnp.concatenate(parts, axis=0).astype(BF16)
            return carry

        lax.fori_loop(0, tiles, step, 0)
        for copy in load_copies:
            copy.wait()

    any_spec = pl.BlockSpec(memory_space=pl.ANY)
    vmem_spec = pl.BlockSpec(memory_space=pltpu.VMEM)
    if not load_gate_up:
        gate, up = in_vmem(gate), in_vmem(up)
    moved = sum(w.size for w in kept) * 2
    outs = pl.pallas_call(
        body,
        out_shape=[jax.ShapeDtypeStruct((2, nb * part, width), BF16)] * n
        + [pltpu.VMEM(w.shape, w.dtype) for w in kept],
        in_specs=[pl.BlockSpec(memory_space=pltpu.SMEM)]
        + [any_spec] * nb
        + [any_spec if load_gate_up else vmem_spec] * 2
        + [any_spec] * len(loads),
        out_specs=[vmem_spec] * (n + len(kept)),
        scratch_shapes=[
            pltpu.VMEM((nb * rows, depth), BF16),
            pltpu.VMEM((nb * rows, tile), F32),
            pltpu.SemaphoreType.DMA((nb,)),
            pltpu.SemaphoreType.DMA((tiles, 2)),
            pltpu.SemaphoreType.DMA((max(1, len(loads)),)),
        ],
        compiler_params=pltpu.CompilerParams(vmem_limit_bytes=10 * MIB),
        cost_estimate=pl.CostEstimate(
            flops=4 * nb * rows * depth * width, bytes_accessed=moved + nb * rows * depth * 2, transcendentals=0
        ),
        name="gate_up",
    )(position, *blocks, gate, up, *loads)
    return outs[:n], outs[n:]


def down_product(position, hidden, down, nb, rows):
    n = len(hidden)
    part = rows // n
    width, depth = down.shape[1], down.shape[0]
    tile = tile_of(width, 512)

    def body(where, *refs):
        pieces, down_ref, outs = refs[:n], refs[n], refs[n + 1:n + 1 + nb]
        left, product, sem = refs[n + 1 + nb:]
        copies = [
            pltpu.make_async_copy(pieces[j], left.at[pl.ds(j * nb * part, nb * part)], sem.at[j]) for j in range(n)
        ]
        for copy in copies:
            copy.start()
        for copy in copies:
            copy.wait()
        position = where[0]

        def step(t, carry):
            columns = pl.ds(pl.multiple_of(t * tile, tile), tile)
            result = jnp.dot(left[...], down_ref[:, columns], preferred_element_type=F32)
            for j in range(n):
                at = lax.rem(position + j, n) * part
                for b in range(nb):
                    first = (j * nb + b) * part
                    product[pl.ds(pl.multiple_of(b * rows + at, part), part), :] = result[first:first + part]
            for b in range(nb):
                outs[b][:, columns] = product[b * rows:(b + 1) * rows, :].astype(BF16)
            return carry

        lax.fori_loop(0, width // tile, step, 0)

    any_spec = pl.BlockSpec(memory_space=pl.ANY)
    vmem_spec = pl.BlockSpec(memory_space=pltpu.VMEM)
    return pl.pallas_call(
        body,
        out_shape=[jax.ShapeDtypeStruct((rows, width), BF16)] * nb,
        in_specs=[pl.BlockSpec(memory_space=pltpu.SMEM)] + [any_spec] * n + [vmem_spec],
        out_specs=[vmem_spec] * nb,
        scratch_shapes=[
            pltpu.VMEM((nb * rows, depth), BF16),
            pltpu.VMEM((nb * rows, tile), F32),
            pltpu.SemaphoreType.DMA((n,)),
        ],
        compiler_params=pltpu.CompilerParams(vmem_limit_bytes=8 * MIB),
        cost_estimate=pl.CostEstimate(
            flops=2 * nb * rows * depth * width, bytes_accessed=nb * rows * width * 2, transcendentals=0
        ),
        name="down_product",
    )(position, *hidden, in_vmem(down))


def add(*terms):
    return functools.reduce(jnp.add, [t.astype(F32) for t in terms])


def shards(sizes, tokens, gate_weight, up_weight, down_weight):
    n = sizes["gz"]
    cores = 2 if sizes["gx"] % 2 == 0 else 1
    ny, nz = sizes["gx"] // cores, sizes["gy"]
    rows = tokens.shape[0]
    position = lax.axis_index("gz").astype(jnp.int32).reshape(1)

    def over_core(value):
        return lax.ppermute(value, "gx", [(i, i ^ 1) for i in range(cores * ny)])

    def over_y(value, by):
        return lax.ppermute(
            value, "gx", [(y * cores + c, (y + by) % ny * cores + c) for y in range(ny) for c in range(cores)]
        )

    def over_z(value, by):
        return lax.ppermute(value, "gy", [(z, (z + by) % nz) for z in range(nz)])

    def over_gz(value, by):
        return lax.ppermute(value, "gz", [(i, (i + by) % n) for i in range(n)])

    blocks = {}
    orders = sorted(range(nz), key=lambda z: (min(z, nz - z), z))
    for dz in orders:
        along_z = over_z(tokens, dz) if dz else tokens
        for dy in range(ny):
            one = over_y(along_z, dy) if dy else along_z
            blocks[dy, dz] = [one] + ([over_core(one)] if cores == 2 else [])

    pieces = [[(dy, 0)] for dy in range(ny)]
    pieces = pieces[:1] + [[(dy, dz) for dy in range(ny)] for dz in orders[1:]] + pieces[1:]

    weights = [gate_weight, up_weight, down_weight]
    hiddens = []
    for index, piece in enumerate(pieces):
        arrays = [block for where in piece for block in blocks[where]]
        sums, kept = gate_up(
            position, arrays, weights[0], weights[1], [down_weight] * (index == 1), n, index == 0
        )
        if index == 0:
            weights[:2] = kept
        if index == 1:
            weights[2:] = kept
        arrived = [over_gz(sums[j], j) for j in range(1, n)]
        both = add(sums[0], *arrived)
        own = (jax.nn.silu(both[0]) * both[1]).astype(BF16)
        hiddens.append([own] + [over_gz(own, -j) for j in range(1, n)])

    totals = {}
    for piece, hidden in zip(pieces, hiddens):
        partial = down_product(position, hidden, weights[2], len(piece) * cores, rows)
        for index, where in enumerate(piece):
            mine = partial[index * cores]
            totals[where] = [mine] + ([over_core(partial[index * cores + 1])] if cores == 2 else [])

    finals = []
    for dz in orders:
        terms = list(totals[0, dz])
        for dy in range(1, ny):
            terms.append(over_y(add(*totals[dy, dz]).astype(BF16), -dy))
        if dz:
            finals.append(over_z(add(*terms).astype(BF16), -dz))
        else:
            finals.extend(terms)
    return add(*finals).astype(BF16)


def solution(mesh):
    sizes = dict(mesh.shape)
    return jax.shard_map(
        functools.partial(shards, sizes),
        mesh=mesh,
        in_specs=(
            P(("gx", "gy"), "gz"),
            P("gz", ("gx", "gy")),
            P("gz", ("gx", "gy")),
            P(("gx", "gy"), "gz"),
        ),
        out_specs=P(("gx", "gy"), "gz"),
        check_vma=False,
    )
```

time: 3180 us -> 276 us (0.09)
  waiting for transfers between devices: 3070 us -> 131 us
  matrix products: 87.2 us -> 0 us
  Pallas kernels: 0 us -> 72.6 us
  starting transfers between devices: 0.46 us -> 36.5 us
    all_gather x5 -> x0, waiting for transfers between devices: 2960 us -> none  [the longest x1 976 us: shards(): lax.all_gather(gate_weight, 'gy', axis=1, tiled=True)]
    ppermute x0 -> x40, waiting for transfers between devices: none -> 131 us  [the longest x10 52.1 us: over_gz(): return lax.ppermute(value, 'gz', [(i, (i + by) % n) for i in range(n)])]
    reduce_scatter x3 -> x0, waiting for transfers between devices: 106 us -> none  [the longest x1 51.3 us: shards(): lax.psum_scatter(up_partial.astype(jnp.bfloat16), 'gz', scatter_dimension...]
    dot_general x3 -> x0, matrix products: 87.2 us -> none  [the longest x2 62.3 us: column_product(): return jnp.dot(gathered, weight_piece, preferred_element_type=jnp.float32)]
    pallas_call x0 -> x10, Pallas kernels: none -> 72.6 us  [the longest x5 45.1 us: gate_up(): pl.pallas_call(body, out_shape=[jax.ShapeDtypeStruct((2, nb * part, width...]
    ppermute x0 -> x40, starting transfers between devices: none -> 36.5 us  [the longest x6 13.3 us: over_z(): return lax.ppermute(value, 'gy', [(z, (z + by) % nz) for z in range(nz)])]
  transfers between devices with their start and end apart: 8 -> 40, of which waited for: 8 -> 16; matrix products, arithmetic and copies ran while one was open for 2% -> 1% of each run, Pallas kernels for 0% -> 26%
where the time goes in v1:
time: 276 us
  waiting for transfers between devices  131 us (47%)
  Pallas kernels  72.6 us (26%)
  starting transfers between devices  36.5 us (13%)
  local copies, waits for them, and re-layouts  31.6 us (11%)
  other arithmetic  4.1 us (1%)
    ppermute x10, waiting for transfers between devices, over_gz(): return lax.ppermute(value, 'gz', [(i, (i + by) % n) for i in range(n)])  52.1 us
    pallas_call x5, Pallas kernels, gate_up(): pl.pallas_call(body, out_shape=[jax.ShapeDtypeStruct((2, nb * part, width...  45.1 us
    ppermute x8, waiting for transfers between devices, over_y(): lax.ppermute(value, 'gx', [(y * cores + c, (y + by) % ny * cores + c) for...  38.9 us
    ppermute x6, waiting for transfers between devices, over_z(): return lax.ppermute(value, 'gy', [(z, (z + by) % nz) for z in range(nz)])  37.9 us
    unnamed x18, local copies, waits for them, and re-layouts  31.6 us
    pallas_call x5, Pallas kernels, down_product(): pl.pallas_call(body, out_shape=[jax.ShapeDtypeStruct((rows, width), BF16)...  27.4 us
    ppermute x6, starting transfers between devices, over_z(): return lax.ppermute(value, 'gy', [(z, (z + by) % nz) for z in range(nz)])  13.3 us
    ppermute x10, starting transfers between devices, over_gz(): return lax.ppermute(value, 'gz', [(i, (i + by) % n) for i in range(n)])  13.3 us
  transfers between devices with their start and end apart: 40, of which 16 were waited for; matrix products, arithmetic and copies ran while one was open for 1% of the time, Pallas kernels for 26%

profile of v1, /device:TPU:0, one launch (start us, length us, event | category | flops | bytes accessed | tf_op | source)
XLA Modules:
  0.0 276.0 jit_solution(16577182521946897694)
XLA Ops:
  0.5 2.5 collective-permute-start.8
  3.0 1.6 collective-permute-start.3
  4.5 2.2 collective-permute-start.20
  6.8 5.2 %copy-done.6 = bf16[4096,1792]{1,0:T(8,128)(2,1)S(1)} copy-done((bf16[4096,1792]{1,0:T(8,128)(2,1)S(1)}, bf16[4096,1792]{1,0:T(8,128)(2,1)}, u32[]{:S(2)}) %copy-start.6) | copy-done | bytes 14680088
  12.0 7.5 %gate_up.5 = (bf16[2,64,1792]{2,1,0:T(8,128)(2,1)S(1)}, bf16[2,64,1792]{2,1,0:T(8,128)(2,1)S(1)}, bf16[4096,1792]{1,0:T(8,128)(2,1)S(1)}, bf16[4096,1792]{1,0:T(8,128)(2,1)S(1)}) custom-call(s32[1]{0:T(128)} %bitcast.refs_0_.where, bf16[64,4096]{1,0:T(8,128)(2,1)} %refs_1_.1, bf16[64,4096]{1,0:T(8,128)(2,1)S(1)} %collective-permute-done.refs_2_, ...), custom_call_target="tpu_custom_call" | custom-call | flops 3758096384 | bytes 30408704 | tf_op jit(solution)/shard_map/gate_up/pallas_call | solution.py:94
  19.5 5.2 %copy-done = bf16[4096,1792]{1,0:T(8,128)(2,1)} copy-done((bf16[4096,1792]{1,0:T(8,128)(2,1)}, bf16[4096,1792]{1,0:T(8,128)(2,1)S(1)}, u32[]{:S(2)}) %copy-start) | copy-done | bytes 14680088
  24.7 1.5 collective-permute-start.1
  26.2 0.8 collective-permute-start.30
  27.5 2.3 collective-permute-done.20.refs_1_
  29.8 7.1 %collective-permute-done.1 = bf16[2,64,1792]{2,1,0:T(8,128)(2,1)S(1)} collective-permute-done((bf16[2,64,1792]{2,1,0:T(8,128)(2,1)S(1)}, bf16[2,64,1792]{2,1,0:T(8,128)(2,1)S(1)}, u32[]{:S(2)}, u32[]{:S(2)}) %collective-permute-start.1) | collective-permute-done | bytes 458784 | tf_op jit(solution)/shard_map/ppermute | solution.py:194
  37.5 5.2 %copy-done.1 = bf16[4096,1792]{1,0:T(8,128)(2,1)S(1)} copy-done((bf16[4096,1792]{1,0:T(8,128)(2,1)S(1)}, bf16[4096,1792]{1,0:T(8,128)(2,1)}, u32[]{:S(2)}) %copy-start.1) | copy-done | bytes 14680088
  42.6 5.8 %gate_up.7 = (bf16[2,64,1792]{2,1,0:T(8,128)(2,1)S(1)}, bf16[2,64,1792]{2,1,0:T(8,128)(2,1)S(1)}) custom-call(s32[1]{0:T(128)} %bitcast.refs_0_.where, bf16[64,4096]{1,0:T(8,128)(2,1)S(1)} %collective-permute-done.8.refs_1_, bf16[64,4096]{1,0:T(8,128)(2,1)S(1)} %collective-permute-done.9.refs_2_, bf16[4096,1792]{1,0:T(8,128)(2,1)S(1)} %copy-done.1, ...), custom_call_target="tpu_custom_call" | custom-call | flops 3758096384 | bytes 1048576 | tf_op jit(solution)/shard_map/gate_up/pallas_call | solution.py:94
  48.4 1.6 collective-permute-start.10
  50.1 2.7 collective-permute-done.30.refs_1_
  53.4 6.3 %collective-permute-done.10 = bf16[2,64,1792]{2,1,0:T(8,128)(2,1)S(1)} collective-permute-done((bf16[2,64,1792]{2,1,0:T(8,128)(2,1)S(1)}, bf16[2,64,1792]{2,1,0:T(8,128)(2,1)S(1)}, u32[]{:S(2)}, u32[]{:S(2)}) %collective-permute-start.10) | collective-permute-done | bytes 458784 | tf_op jit(solution)/shard_map/ppermute | solution.py:194
  60.5 1.3 collective-permute-start.2
  61.8 5.4 %collective-permute-done.32.refs_3_ = bf16[64,4096]{1,0:T(8,128)(2,1)S(1)} collective-permute-done((bf16[64,4096]{1,0:T(8,128)(2,1)S(1)}, bf16[64,4096]{1,0:T(8,128)(2,1)S(1)}, u32[]{:S(2)}, u32[]{:S(2)}) %collective-permute-start.32) | collective-permute-done | bytes 524320 | tf_op jit(solution)/shard_map/ppermute | solution.py:186
  68.0 5.2 %copy-done.2 = bf16[4096,1792]{1,0:T(8,128)(2,1)S(1)} copy-done((bf16[4096,1792]{1,0:T(8,128)(2,1)S(1)}, bf16[4096,1792]{1,0:T(8,128)(2,1)}, u32[]{:S(2)}) %copy-start.2) | copy-done | bytes 14680088
  73.2 5.2 %copy-done.5 = bf16[4096,1792]{1,0:T(8,128)(2,1)S(1)} copy-done((bf16[4096,1792]{1,0:T(8,128)(2,1)S(1)}, bf16[4096,1792]{1,0:T(8,128)(2,1)}, u32[]{:S(2)}) %copy-start.5) | copy-done | bytes 14680088
  78.3 12.1 %gate_up.6 = (bf16[2,128,1792]{2,1,0:T(8,128)(2,1)}, bf16[2,128,1792]{2,1,0:T(8,128)(2,1)}, bf16[1792,4096]{1,0:T(8,128)(2,1)S(1)}) custom-call(s32[1]{0:T(128)} %bitcast.refs_0_.where, bf16[64,4096]{1,0:T(8,128)(2,1)S(1)} %collective-permute-done.3.refs_1_, bf16[64,4096]{1,0:T(8,128)(2,1)S(1)} %collective-permute-done.4.refs_2_, ...), custom_call_target="tpu_custom_call" | custom-call | flops 7516192768 | bytes 16777216 | tf_op jit(solution)/shard_map/gate_up/pallas_call | solution.py:94
  90.4 1.6 collective-permute-start.11
  92.5 9.9 %gate_up.8 = (bf16[2,128,1792]{2,1,0:T(8,128)(2,1)S(1)}, bf16[2,128,1792]{2,1,0:T(8,128)(2,1)S(1)}) custom-call(s32[1]{0:T(128)} %bitcast.refs_0_.where, bf16[64,4096]{1,0:T(8,128)(2,1)S(1)} %collective-permute-done.20.refs_1_, bf16[64,4096]{1,0:T(8,128)(2,1)S(1)} %collective-permute-done.21.refs_2_, bf16[64,4096]{1,0:T(8,128)(2,1)S(1)} %collective-permute-done.22.refs_3_, ...), custom_call_target="tpu_custom_call" | custom-call | flops 7516192768 | bytes 2097152 | tf_op jit(solution)/shard_map/gate_up/pallas_call | solution.py:94
  102.4 1.6 collective-permute-start.24
  104.0 4.2 %down_product.6 = (bf16[64,4096]{1,0:T(8,128)(2,1)S(1)}, bf16[64,4096]{1,0:T(8,128)(2,1)S(1)}) custom-call(s32[1]{0:T(128)} %bitcast.refs_0_.where, bf16[64,1792]{1,0:T(8,128)(2,1)S(1)} %fusion.7.refs_0_, bf16[64,1792]{1,0:T(8,128)(2,1)S(1)} %collective-permute-done.11.refs_1_, bf16[1792,4096]{1,0:T(8,128)(2,1)S(1)} %get-tuple-element.38.refs_2_), custom_call_target="tpu_custom_call" | custom-call | flops 1879048192 | bytes 1048576 | tf_op jit(solution)/shard_map/down_product/pallas_call | solution.py:153
  108.4 5.2 %copy-done.3 = bf16[4096,1792]{1,0:T(8,128)(2,1)S(1)} copy-done((bf16[4096,1792]{1,0:T(8,128)(2,1)S(1)}, bf16[4096,1792]{1,0:T(8,128)(2,1)}, u32[]{:S(2)}) %copy-start.3) | copy-done | bytes 14680088
  113.6 9.9 %gate_up.9 = (bf16[2,128,1792]{2,1,0:T(8,128)(2,1)S(1)}, bf16[2,128,1792]{2,1,0:T(8,128)(2,1)S(1)}) custom-call(s32[1]{0:T(128)} %bitcast.refs_0_.where, bf16[64,4096]{1,0:T(8,128)(2,1)S(1)} %collective-permute-done.30.refs_1_, bf16[64,4096]{1,0:T(8,128)(2,1)S(1)} %collective-permute-done.31.refs_2_, bf16[64,4096]{1,0:T(8,128)(2,1)S(1)} %collective-permute-done.32.refs_3_, ...), custom_call_target="tpu_custom_call" | custom-call | flops 7516192768 | bytes 2097152 | tf_op jit(solution)/shard_map/gate_up/pallas_call | solution.py:94
  124.1 4.3 %down_product.5 = (bf16[64,4096]{1,0:T(8,128)(2,1)S(1)}, bf16[64,4096]{1,0:T(8,128)(2,1)S(1)}) custom-call(s32[1]{0:T(128)} %bitcast.refs_0_.where, bf16[64,1792]{1,0:T(8,128)(2,1)S(1)} %fusion.9.refs_0_, bf16[64,1792]{1,0:T(8,128)(2,1)S(1)} %collective-permute-done.2.refs_1_, bf16[1792,4096]{1,0:T(8,128)(2,1)S(1)} %get-tuple-element.38.refs_2_), custom_call_target="tpu_custom_call" | custom-call | flops 1879048192 | bytes 1048576 | tf_op jit(solution)/shard_map/down_product/pallas_call | solution.py:153
  130.0 1.5 collective-permute-start.15
  131.5 6.7 %collective-permute-done.24 = bf16[2,128,1792]{2,1,0:T(8,128)(2,1)S(1)} collective-permute-done((bf16[2,128,1792]{2,1,0:T(8,128)(2,1)S(1)}, bf16[2,128,1792]{2,1,0:T(8,128)(2,1)S(1)}, u32[]{:S(2)}, u32[]{:S(2)}) %collective-permute-start.24) | collective-permute-done | bytes 917536 | tf_op jit(solution)/shard_map/ppermute | solution.py:194
  138.7 1.6 collective-permute-start.25
  140.3 17.6 %collective-permute-done.34 = bf16[2,128,1792]{2,1,0:T(8,128)(2,1)S(1)} collective-permute-done((bf16[2,128,1792]{2,1,0:T(8,128)(2,1)S(1)}, bf16[2,128,1792]{2,1,0:T(8,128)(2,1)S(1)}, u32[]{:S(2)}, u32[]{:S(2)}) %collective-permute-start.34) | collective-permute-done | bytes 917536 | tf_op jit(solution)/shard_map/ppermute | solution.py:194
  158.4 1.6 collective-permute-start.35
  159.9 7.8 %collective-permute-done.15.refs_1_ = bf16[128,1792]{1,0:T(8,128)(2,1)S(1)} collective-permute-done((bf16[128,1792]{1,0:T(8,128)(2,1)S(1)}, bf16[128,1792]{1,0:T(8,128)(2,1)S(1)}, u32[]{:S(2)}, u32[]{:S(2)}) %collective-permute-start.15) | collective-permute-done | bytes 458784 | tf_op jit(solution)/shard_map/ppermute | solution.py:194
  167.7 6.3 %down_product.7 = (bf16[64,4096]{1,0:T(8,128)(2,1)S(1)}, bf16[64,4096]{1,0:T(8,128)(2,1)S(1)}, bf16[64,4096]{1,0:T(8,128)(2,1)S(1)}, bf16[64,4096]{1,0:T(8,128)(2,1)S(1)}) custom-call(s32[1]{0:T(128)} %bitcast.refs_0_.where, bf16[128,1792]{1,0:T(8,128)(2,1)S(1)} %fusion.5.refs_0_, bf16[128,1792]{1,0:T(8,128)(2,1)S(1)} %collective-permute-done.15.refs_1_, ...), custom_call_target="tpu_custom_call" | custom-call | flops 3758096384 | bytes 2097152 | tf_op jit(solution)/shard_map/down_product/pallas_call | solution.py:153
  174.1 3.4 %collective-permute-done.25.refs_1_ = bf16[128,1792]{1,0:T(8,128)(2,1)S(1)} collective-permute-done((bf16[128,1792]{1,0:T(8,128)(2,1)S(1)}, bf16[128,1792]{1,0:T(8,128)(2,1)S(1)}, u32[]{:S(2)}, u32[]{:S(2)}) %collective-permute-start.25) | collective-permute-done | bytes 458784 | tf_op jit(solution)/shard_map/ppermute | solution.py:194
  177.6 6.3 %down_product.8 = (bf16[64,4096]{1,0:T(8,128)(2,1)S(1)}, bf16[64,4096]{1,0:T(8,128)(2,1)S(1)}, bf16[64,4096]{1,0:T(8,128)(2,1)S(1)}, bf16[64,4096]{1,0:T(8,128)(2,1)S(1)}) custom-call(s32[1]{0:T(128)} %bitcast.refs_0_.where, bf16[128,1792]{1,0:T(8,128)(2,1)S(1)} %fusion.3.refs_0_, bf16[128,1792]{1,0:T(8,128)(2,1)S(1)} %collective-permute-done.25.refs_1_, ...), custom_call_target="tpu_custom_call" | custom-call | flops 3758096384 | bytes 2097152 | tf_op jit(solution)/shard_map/down_product/pallas_call | solution.py:153
  183.9 3.1 %collective-permute-done.35.refs_1_ = bf16[128,1792]{1,0:T(8,128)(2,1)S(1)} collective-permute-done((bf16[128,1792]{1,0:T(8,128)(2,1)S(1)}, bf16[128,1792]{1,0:T(8,128)(2,1)S(1)}, u32[]{:S(2)}, u32[]{:S(2)}) %collective-permute-start.35) | collective-permute-done | bytes 458784 | tf_op jit(solution)/shard_map/ppermute | solution.py:194
  187.0 6.3 %down_product.9 = (bf16[64,4096]{1,0:T(8,128)(2,1)S(1)}, bf16[64,4096]{1,0:T(8,128)(2,1)S(1)}, bf16[64,4096]{1,0:T(8,128)(2,1)S(1)}, bf16[64,4096]{1,0:T(8,128)(2,1)S(1)}) custom-call(s32[1]{0:T(128)} %bitcast.refs_0_.where, bf16[128,1792]{1,0:T(8,128)(2,1)S(1)} %fusion.1.refs_0_, bf16[128,1792]{1,0:T(8,128)(2,1)S(1)} %collective-permute-done.35.refs_1_, ...), custom_call_target="tpu_custom_call" | custom-call | flops 3758096384 | bytes 2097152 | tf_op jit(solution)/shard_map/down_product/pallas_call | solution.py:153
  194.3 1.9 collective-permute-done.37
  197.0 13.4 %collective-permute-done.18 = bf16[64,4096]{1,0:T(8,128)(2,1)S(1)} collective-permute-done((bf16[64,4096]{1,0:T(8,128)(2,1)S(1)}, bf16[64,4096]{1,0:T(8,128)(2,1)S(1)}, u32[]{:S(2)}, u32[]{:S(2)}) %collective-permute-start.18) | collective-permute-done | bytes 524320 | tf_op jit(solution)/shard_map/ppermute | solution.py:186
  211.1 1.6 collective-permute-start.38
  212.7 12.6 %collective-permute-done.28 = bf16[64,4096]{1,0:T(8,128)(2,1)S(1)} collective-permute-done((bf16[64,4096]{1,0:T(8,128)(2,1)S(1)}, bf16[64,4096]{1,0:T(8,128)(2,1)S(1)}, u32[]{:S(2)}, u32[]{:S(2)}) %collective-permute-start.28) | collective-permute-done | bytes 524320 | tf_op jit(solution)/shard_map/ppermute | solution.py:186
  225.2 1.7 collective-permute-start.19
  227.5 7.5 %collective-permute-done.38 = bf16[64,4096]{1,0:T(8,128)(2,1)S(1)} collective-permute-done((bf16[64,4096]{1,0:T(8,128)(2,1)S(1)}, bf16[64,4096]{1,0:T(8,128)(2,1)S(1)}, u32[]{:S(2)}, u32[]{:S(2)}) %collective-permute-start.38) | collective-permute-done | bytes 524320 | tf_op jit(solution)/shard_map/ppermute | solution.py:186
  235.2 6.6 %collective-permute-start.39 = (bf16[64,4096]{1,0:T(8,128)(2,1)S(1)}, bf16[64,4096]{1,0:T(8,128)(2,1)S(1)}, u32[]{:S(2)}, u32[]{:S(2)}) collective-permute-start(bf16[64,4096]{1,0:T(8,128)(2,1)S(1)} %add_convert_fusion.1), channel_id=1, source_target_pairs={{0,4},{2,6},{4,0},{6,2},{1,5},{3,7},{5,1},{7,3},{8,12},{10,14},{12... | collective-permute-start | bytes 1572872 | tf_op jit(solution)/shard_map/ppermute | solution.py:191
  241.8 15.6 %collective-permute-done.29 = bf16[64,4096]{1,0:T(8,128)(2,1)S(1)} collective-permute-done((bf16[64,4096]{1,0:T(8,128)(2,1)S(1)}, bf16[64,4096]{1,0:T(8,128)(2,1)S(1)}, u32[]{:S(2)}, u32[]{:S(2)}) %collective-permute-start.29) | collective-permute-done | bytes 524320 | tf_op jit(solution)/shard_map/ppermute | solution.py:191
  257.4 17.3 %collective-permute-done.39 = bf16[64,4096]{1,0:T(8,128)(2,1)S(1)} collective-permute-done((bf16[64,4096]{1,0:T(8,128)(2,1)S(1)}, bf16[64,4096]{1,0:T(8,128)(2,1)S(1)}, u32[]{:S(2)}, u32[]{:S(2)}) %collective-permute-start.39) | collective-permute-done | bytes 524320 | tf_op jit(solution)/shard_map/ppermute | solution.py:191
  274.8 1.2 add_convert_fusion
  (78 shorter events, 10.8 us)
Async XLA Ops:
  0.0 6.8 %collective-permute-start = (bf16[64,4096]{1,0:T(8,128)(2,1)}, bf16[64,4096]{1,0:T(8,128)(2,1)S(1)}, u32[]{:S(2)}, u32[]{:S(2)}) collective-permute-start(bf16[64,4096]{1,0:T(8,128)(2,1)} %refs_1_.1), channel_id=1, source_target_pairs={{0,8},{8,0},{16,24},{24,16},{1,9},{9,1},{17,25},{25,17},{2,10},{10... | collective-permute-start | bytes 1572872 | tf_op jit(solution)/shard_map/ppermute | solution.py:183
  0.5 25.7 %collective-permute-start.8 = (bf16[64,4096]{1,0:T(8,128)(2,1)}, bf16[64,4096]{1,0:T(8,128)(2,1)S(1)}, u32[]{:S(2)}, u32[]{:S(2)}) collective-permute-start(bf16[64,4096]{1,0:T(8,128)(2,1)} %refs_1_.1), channel_id=1, source_target_pairs={{0,16},{8,24},{16,0},{24,8},{1,17},{9,25},{17,1},{25,9},{2,18},{10... | collective-permute-start | bytes 1572872 | tf_op jit(solution)/shard_map/ppermute | solution.py:186
  3.0 24.0 %collective-permute-start.3 = (bf16[64,4096]{1,0:T(8,128)(2,1)}, bf16[64,4096]{1,0:T(8,128)(2,1)S(1)}, u32[]{:S(2)}, u32[]{:S(2)}) collective-permute-start(bf16[64,4096]{1,0:T(8,128)(2,1)} %refs_1_.1), channel_id=1, source_target_pairs={{0,2},{2,4},{4,6},{6,0},{1,3},{3,5},{5,7},{7,1},{8,10},{10,12},{12... | collective-permute-start | bytes 1572872 | tf_op jit(solution)/shard_map/ppermute | solution.py:191
  4.5 25.2 %collective-permute-start.20 = (bf16[64,4096]{1,0:T(8,128)(2,1)}, bf16[64,4096]{1,0:T(8,128)(2,1)S(1)}, u32[]{:S(2)}, u32[]{:S(2)}) collective-permute-start(bf16[64,4096]{1,0:T(8,128)(2,1)} %refs_1_.1), channel_id=1, source_target_pairs={{0,6},{2,0},{4,2},{6,4},{1,7},{3,1},{5,3},{7,5},{8,14},{10,8},{12,... | collective-permute-start | bytes 1572872 | tf_op jit(solution)/shard_map/ppermute | solution.py:191
  6.8 5.2 %copy-start.6 = (bf16[4096,1792]{1,0:T(8,128)(2,1)S(1)}, bf16[4096,1792]{1,0:T(8,128)(2,1)}, u32[]{:S(2)}) copy-start(bf16[4096,1792]{1,0:T(8,128)(2,1)} %refs_3_.1) | copy-start | bytes 44040196
  19.5 5.2 %copy-start = (bf16[4096,1792]{1,0:T(8,128)(2,1)}, bf16[4096,1792]{1,0:T(8,128)(2,1)S(1)}, u32[]{:S(2)}) copy-start(bf16[4096,1792]{1,0:T(8,128)(2,1)S(1)} %get-tuple-element.36.refs_5_.refs_3_) | copy-start | bytes 44040196
  24.7 23.7 %copy-start.4 = (bf16[4096,1792]{1,0:T(8,128)(2,1)}, bf16[4096,1792]{1,0:T(8,128)(2,1)S(1)}, u32[]{:S(2)}) copy-start(bf16[4096,1792]{1,0:T(8,128)(2,1)S(1)} %get-tuple-element.37.refs_6_.refs_4_) | copy-start | bytes 44040196
  24.7 12.2 %collective-permute-start.1 = (bf16[2,64,1792]{2,1,0:T(8,128)(2,1)S(1)}, bf16[2,64,1792]{2,1,0:T(8,128)(2,1)S(1)}, u32[]{:S(2)}, u32[]{:S(2)}) collective-permute-start(bf16[2,64,1792]{2,1,0:T(8,128)(2,1)S(1)} %get-tuple-element.35), channel_id=1, source_target_pairs={{0,1},{1,0},{2,3},{3,2},{4,5},{5,4},{6,7},{7,6},{8,9},{9,8},{10,11... | collective-permute-start | bytes 1376264 | tf_op jit(solution)/shard_map/ppermute | solution.py:194
  26.2 11.3 %collective-permute-start.9 = (bf16[64,4096]{1,0:T(8,128)(2,1)S(1)}, bf16[64,4096]{1,0:T(8,128)(2,1)S(1)}, u32[]{:S(2)}, u32[]{:S(2)}) collective-permute-start(bf16[64,4096]{1,0:T(8,128)(2,1)S(1)} %collective-permute-done.8.refs_1_), channel_id=1, source_target_pairs={{0,8},{8,0},{16,24},{24,16},{1,9},{9,1},{17,25},{25,17},{2,10},{10... | collective-permute-start | bytes 1572872 | tf_op jit(solution)/shard_map/ppermute | solution.py:183
  26.2 26.7 %collective-permute-start.30 = (bf16[64,4096]{1,0:T(8,128)(2,1)}, bf16[64,4096]{1,0:T(8,128)(2,1)S(1)}, u32[]{:S(2)}, u32[]{:S(2)}) collective-permute-start(bf16[64,4096]{1,0:T(8,128)(2,1)} %refs_1_.1), channel_id=1, source_target_pairs={{0,4},{2,6},{4,0},{6,2},{1,5},{3,7},{5,1},{7,3},{8,12},{10,14},{12... | collective-permute-start | bytes 1572872 | tf_op jit(solution)/shard_map/ppermute | solution.py:191
  27.0 25.9 %collective-permute-start.5 = (bf16[64,4096]{1,0:T(8,128)(2,1)S(1)}, bf16[64,4096]{1,0:T(8,128)(2,1)S(1)}, u32[]{:S(2)}, u32[]{:S(2)}) collective-permute-start(bf16[64,4096]{1,0:T(8,128)(2,1)S(1)} %collective-permute-done.3.refs_1_), channel_id=1, source_target_pairs={{0,16},{8,24},{16,0},{24,8},{1,17},{9,25},{17,1},{25,9},{2,18},{10... | collective-permute-start | bytes 1572872 | tf_op jit(solution)/shard_map/ppermute | solution.py:186
  29.8 30.2 %collective-permute-start.4 = (bf16[64,4096]{1,0:T(8,128)(2,1)S(1)}, bf16[64,4096]{1,0:T(8,128)(2,1)S(1)}, u32[]{:S(2)}, u32[]{:S(2)}) collective-permute-start(bf16[64,4096]{1,0:T(8,128)(2,1)S(1)} %collective-permute-done.3.refs_1_), channel_id=1, source_target_pairs={{0,8},{8,0},{16,24},{24,16},{1,9},{9,1},{17,25},{25,17},{2,10},{10... | collective-permute-start | bytes 1572872 | tf_op jit(solution)/shard_map/ppermute | solution.py:183
  36.8 23.7 %collective-permute-start.22 = (bf16[64,4096]{1,0:T(8,128)(2,1)S(1)}, bf16[64,4096]{1,0:T(8,128)(2,1)S(1)}, u32[]{:S(2)}, u32[]{:S(2)}) collective-permute-start(bf16[64,4096]{1,0:T(8,128)(2,1)S(1)} %collective-permute-done.20.refs_1_), channel_id=1, source_target_pairs={{0,16},{8,24},{16,0},{24,8},{1,17},{9,25},{17,1},{25,9},{2,18},{10... | collective-permute-start | bytes 1572872 | tf_op jit(solution)/shard_map/ppermute | solution.py:186
  37.4 5.2 %copy-start.1 = (bf16[4096,1792]{1,0:T(8,128)(2,1)S(1)}, bf16[4096,1792]{1,0:T(8,128)(2,1)}, u32[]{:S(2)}) copy-start(bf16[4096,1792]{1,0:T(8,128)(2,1)} %copy-done) | copy-start | bytes 44040196
  48.4 11.3 %collective-permute-start.10 = (bf16[2,64,1792]{2,1,0:T(8,128)(2,1)S(1)}, bf16[2,64,1792]{2,1,0:T(8,128)(2,1)S(1)}, u32[]{:S(2)}, u32[]{:S(2)}) collective-permute-start(bf16[2,64,1792]{2,1,0:T(8,128)(2,1)S(1)} %get-tuple-element.42), channel_id=1, source_target_pairs={{0,1},{1,0},{2,3},{3,2},{4,5},{5,4},{6,7},{7,6},{8,9},{9,8},{10,11... | collective-permute-start | bytes 1376264 | tf_op jit(solution)/shard_map/ppermute | solution.py:194
  52.8 37.6 %collective-permute-start.21 = (bf16[64,4096]{1,0:T(8,128)(2,1)S(1)}, bf16[64,4096]{1,0:T(8,128)(2,1)S(1)}, u32[]{:S(2)}, u32[]{:S(2)}) collective-permute-start(bf16[64,4096]{1,0:T(8,128)(2,1)S(1)} %collective-permute-done.20.refs_1_), channel_id=1, source_target_pairs={{0,8},{8,0},{16,24},{24,16},{1,9},{9,1},{17,25},{25,17},{2,10},{10... | collective-permute-start | bytes 1572872 | tf_op jit(solution)/shard_map/ppermute | solution.py:183
  52.9 14.3 %collective-permute-start.32 = (bf16[64,4096]{1,0:T(8,128)(2,1)S(1)}, bf16[64,4096]{1,0:T(8,128)(2,1)S(1)}, u32[]{:S(2)}, u32[]{:S(2)}) collective-permute-start(bf16[64,4096]{1,0:T(8,128)(2,1)S(1)} %collective-permute-done.30.refs_1_), channel_id=1, source_target_pairs={{0,16},{8,24},{16,0},{24,8},{1,17},{9,25},{17,1},{25,9},{2,18},{10... | collective-permute-start | bytes 1572872 | tf_op jit(solution)/shard_map/ppermute | solution.py:186
  59.7 7.5 %collective-permute-start.6 = (bf16[64,4096]{1,0:T(8,128)(2,1)S(1)}, bf16[64,4096]{1,0:T(8,128)(2,1)S(1)}, u32[]{:S(2)}, u32[]{:S(2)}) collective-permute-start(bf16[64,4096]{1,0:T(8,128)(2,1)S(1)} %collective-permute-done.5.refs_3_), channel_id=1, source_target_pairs={{0,8},{8,0},{16,24},{24,16},{1,9},{9,1},{17,25},{25,17},{2,10},{10... | collective-permute-start | bytes 1572872 | tf_op jit(solution)/shard_map/ppermute | solution.py:183
  59.9 48.4 %collective-permute-start.31 = (bf16[64,4096]{1,0:T(8,128)(2,1)S(1)}, bf16[64,4096]{1,0:T(8,128)(2,1)S(1)}, u32[]{:S(2)}, u32[]{:S(2)}) collective-permute-start(bf16[64,4096]{1,0:T(8,128)(2,1)S(1)} %collective-permute-done.30.refs_1_), channel_id=1, source_target_pairs={{0,8},{8,0},{16,24},{24,16},{1,9},{9,1},{17,25},{25,17},{2,10},{10... | collective-permute-start | bytes 1572872 | tf_op jit(solution)/shard_map/ppermute | solution.py:183
  60.5 63.6 %collective-permute-start.2 = (bf16[64,1792]{1,0:T(8,128)(2,1)S(1)}, bf16[64,1792]{1,0:T(8,128)(2,1)S(1)}, u32[]{:S(2)}, u32[]{:S(2)}) collective-permute-start(bf16[64,1792]{1,0:T(8,128)(2,1)S(1)} %fusion.9.refs_0_), channel_id=1, source_target_pairs={{0,1},{1,0},{2,3},{3,2},{4,5},{5,4},{6,7},{7,6},{8,9},{9,8},{10,11... | collective-permute-start | bytes 688136 | tf_op jit(solution)/shard_map/ppermute | solution.py:194
  67.2 24.8 %collective-permute-start.23 = (bf16[64,4096]{1,0:T(8,128)(2,1)S(1)}, bf16[64,4096]{1,0:T(8,128)(2,1)S(1)}, u32[]{:S(2)}, u32[]{:S(2)}) collective-permute-start(bf16[64,4096]{1,0:T(8,128)(2,1)S(1)} %collective-permute-done.22.refs_3_), channel_id=1, source_target_pairs={{0,8},{8,0},{16,24},{24,16},{1,9},{9,1},{17,25},{25,17},{2,10},{10... | collective-permute-start | bytes 1572872 | tf_op jit(solution)/shard_map/ppermute | solution.py:183
  67.2 41.2 %collective-permute-start.33 = (bf16[64,4096]{1,0:T(8,128)(2,1)S(1)}, bf16[64,4096]{1,0:T(8,128)(2,1)S(1)}, u32[]{:S(2)}, u32[]{:S(2)}) collective-permute-start(bf16[64,4096]{1,0:T(8,128)(2,1)S(1)} %collective-permute-done.32.refs_3_), channel_id=1, source_target_pairs={{0,8},{8,0},{16,24},{24,16},{1,9},{9,1},{17,25},{25,17},{2,10},{10... | collective-permute-start | bytes 1572872 | tf_op jit(solution)/shard_map/ppermute | solution.py:183
  68.0 5.2 %copy-start.2 = (bf16[4096,1792]{1,0:T(8,128)(2,1)S(1)}, bf16[4096,1792]{1,0:T(8,128)(2,1)}, u32[]{:S(2)}) copy-start(bf16[4096,1792]{1,0:T(8,128)(2,1)} %copy-done) | copy-start | bytes 44040196
  73.2 5.2 %copy-start.5 = (bf16[4096,1792]{1,0:T(8,128)(2,1)S(1)}, bf16[4096,1792]{1,0:T(8,128)(2,1)}, u32[]{:S(2)}) copy-start(bf16[4096,1792]{1,0:T(8,128)(2,1)} %copy-done.4) | copy-start | bytes 44040196
  90.4 12.0 %collective-permute-start.11 = (bf16[64,1792]{1,0:T(8,128)(2,1)S(1)}, bf16[64,1792]{1,0:T(8,128)(2,1)S(1)}, u32[]{:S(2)}, u32[]{:S(2)}) collective-permute-start(bf16[64,1792]{1,0:T(8,128)(2,1)S(1)} %fusion.7.refs_0_), channel_id=1, source_target_pairs={{0,1},{1,0},{2,3},{3,2},{4,5},{5,4},{6,7},{7,6},{8,9},{9,8},{10,11... | collective-permute-start | bytes 688136 | tf_op jit(solution)/shard_map/ppermute | solution.py:194
  92.0 37.2 %collective-permute-start.14 = (bf16[2,128,1792]{2,1,0:T(8,128)(2,1)}, bf16[2,128,1792]{2,1,0:T(8,128)(2,1)S(1)}, u32[]{:S(2)}, u32[]{:S(2)}) collective-permute-start(bf16[2,128,1792]{2,1,0:T(8,128)(2,1)} %get-tuple-element.46), channel_id=1, source_target_pairs={{0,1},{1,0},{2,3},{3,2},{4,5},{5,4},{6,7},{7,6},{8,9},{9,8},{10,11... | collective-permute-start | bytes 2752520 | tf_op jit(solution)/shard_map/ppermute | solution.py:194
  102.4 35.8 %collective-permute-start.24 = (bf16[2,128,1792]{2,1,0:T(8,128)(2,1)S(1)}, bf16[2,128,1792]{2,1,0:T(8,128)(2,1)S(1)}, u32[]{:S(2)}, u32[]{:S(2)}) collective-permute-start(bf16[2,128,1792]{2,1,0:T(8,128)(2,1)S(1)} %get-tuple-element.52), channel_id=1, source_target_pairs={{0,1},{1,0},{2,3},{3,2},{4,5},{5,4},{6,7},{7,6},{8,9},{9,8},{10,11... | collective-permute-start | bytes 2752520 | tf_op jit(solution)/shard_map/ppermute | solution.py:194
  108.3 20.3 %collective-permute-start.12 = (bf16[64,4096]{1,0:T(8,128)(2,1)S(1)}, bf16[64,4096]{1,0:T(8,128)(2,1)S(1)}, u32[]{:S(2)}, u32[]{:S(2)}) collective-permute-start(bf16[64,4096]{1,0:T(8,128)(2,1)S(1)} %get-tuple-element.44), channel_id=1, source_target_pairs={{0,8},{8,0},{16,24},{24,16},{1,9},{9,1},{17,25},{25,17},{2,10},{10... | collective-permute-start | bytes 1572872 | tf_op jit(solution)/shard_map/ppermute | solution.py:183
  108.4 5.2 %copy-start.3 = (bf16[4096,1792]{1,0:T(8,128)(2,1)S(1)}, bf16[4096,1792]{1,0:T(8,128)(2,1)}, u32[]{:S(2)}) copy-start(bf16[4096,1792]{1,0:T(8,128)(2,1)} %copy-done) | copy-start | bytes 44040196
  123.4 34.5 %collective-permute-start.34 = (bf16[2,128,1792]{2,1,0:T(8,128)(2,1)S(1)}, bf16[2,128,1792]{2,1,0:T(8,128)(2,1)S(1)}, u32[]{:S(2)}, u32[]{:S(2)}) collective-permute-start(bf16[2,128,1792]{2,1,0:T(8,128)(2,1)S(1)} %get-tuple-element.58), channel_id=1, source_target_pairs={{0,1},{1,0},{2,3},{3,2},{4,5},{5,4},{6,7},{7,6},{8,9},{9,8},{10,11... | collective-permute-start | bytes 2752520 | tf_op jit(solution)/shard_map/ppermute | solution.py:194
  128.4 1.2 copy-start.7
  128.4 113.5 %collective-permute-start.7 = (bf16[64,4096]{1,0:T(8,128)(2,1)S(1)}, bf16[64,4096]{1,0:T(8,128)(2,1)S(1)}, u32[]{:S(2)}, u32[]{:S(2)}) collective-permute-start(bf16[64,4096]{1,0:T(8,128)(2,1)S(1)} %get-tuple-element.40), channel_id=1, source_target_pairs={{0,8},{8,0},{16,24},{24,16},{1,9},{9,1},{17,25},{25,17},{2,10},{10... | collective-permute-start | bytes 1572872 | tf_op jit(solution)/shard_map/ppermute | solution.py:183
  128.7 113.1 %collective-permute-start.13 = (bf16[64,4096]{1,0:T(8,128)(2,1)S(1)}, bf16[64,4096]{1,0:T(8,128)(2,1)S(1)}, u32[]{:S(2)}, u32[]{:S(2)}) collective-permute-start(bf16[64,4096]{1,0:T(8,128)(2,1)S(1)} %add_convert_fusion.7), channel_id=1, source_target_pairs={{0,16},{8,24},{16,0},{24,8},{1,17},{9,25},{17,1},{25,9},{2,18},{10... | collective-permute-start | bytes 1572872 | tf_op jit(solution)/shard_map/ppermute | solution.py:186
  130.0 37.7 %collective-permute-start.15 = (bf16[128,1792]{1,0:T(8,128)(2,1)S(1)}, bf16[128,1792]{1,0:T(8,128)(2,1)S(1)}, u32[]{:S(2)}, u32[]{:S(2)}) collective-permute-start(bf16[128,1792]{1,0:T(8,128)(2,1)S(1)} %fusion.5.refs_0_), channel_id=1, source_target_pairs={{0,1},{1,0},{2,3},{3,2},{4,5},{5,4},{6,7},{7,6},{8,9},{9,8},{10,11... | collective-permute-start | bytes 1376264 | tf_op jit(solution)/shard_map/ppermute | solution.py:194
  138.7 38.9 %collective-permute-start.25 = (bf16[128,1792]{1,0:T(8,128)(2,1)S(1)}, bf16[128,1792]{1,0:T(8,128)(2,1)S(1)}, u32[]{:S(2)}, u32[]{:S(2)}) collective-permute-start(bf16[128,1792]{1,0:T(8,128)(2,1)S(1)} %fusion.3.refs_0_), channel_id=1, source_target_pairs={{0,1},{1,0},{2,3},{3,2},{4,5},{5,4},{6,7},{7,6},{8,9},{9,8},{10,11... | collective-permute-start | bytes 1376264 | tf_op jit(solution)/shard_map/ppermute | solution.py:194
  158.4 28.7 %collective-permute-start.35 = (bf16[128,1792]{1,0:T(8,128)(2,1)S(1)}, bf16[128,1792]{1,0:T(8,128)(2,1)S(1)}, u32[]{:S(2)}, u32[]{:S(2)}) collective-permute-start(bf16[128,1792]{1,0:T(8,128)(2,1)S(1)} %fusion.1.refs_0_), channel_id=1, source_target_pairs={{0,1},{1,0},{2,3},{3,2},{4,5},{5,4},{6,7},{7,6},{8,9},{9,8},{10,11... | collective-permute-start | bytes 1376264 | tf_op jit(solution)/shard_map/ppermute | solution.py:194
  174.0 19.3 %collective-permute-start.17 = (bf16[64,4096]{1,0:T(8,128)(2,1)S(1)}, bf16[64,4096]{1,0:T(8,128)(2,1)S(1)}, u32[]{:S(2)}, u32[]{:S(2)}) collective-permute-start(bf16[64,4096]{1,0:T(8,128)(2,1)S(1)} %get-tuple-element.50), channel_id=1, source_target_pairs={{0,8},{8,0},{16,24},{24,16},{1,9},{9,1},{17,25},{25,17},{2,10},{10... | collective-permute-start | bytes 1572872 | tf_op jit(solution)/shard_map/ppermute | solution.py:183
  177.6 19.3 %collective-permute-start.16 = (bf16[64,4096]{1,0:T(8,128)(2,1)S(1)}, bf16[64,4096]{1,0:T(8,128)(2,1)S(1)}, u32[]{:S(2)}, u32[]{:S(2)}) collective-permute-start(bf16[64,4096]{1,0:T(8,128)(2,1)S(1)} %get-tuple-element.48), channel_id=1, source_target_pairs={{0,8},{8,0},{16,24},{24,16},{1,9},{9,1},{17,25},{25,17},{2,10},{10... | collective-permute-start | bytes 1572872 | tf_op jit(solution)/shard_map/ppermute | solution.py:183
  187.0 7.0 %collective-permute-start.27 = (bf16[64,4096]{1,0:T(8,128)(2,1)S(1)}, bf16[64,4096]{1,0:T(8,128)(2,1)S(1)}, u32[]{:S(2)}, u32[]{:S(2)}) collective-permute-start(bf16[64,4096]{1,0:T(8,128)(2,1)S(1)} %get-tuple-element.56), channel_id=1, source_target_pairs={{0,8},{8,0},{16,24},{24,16},{1,9},{9,1},{17,25},{25,17},{2,10},{10... | collective-permute-start | bytes 1572872 | tf_op jit(solution)/shard_map/ppermute | solution.py:183
  193.3 17.8 %collective-permute-start.26 = (bf16[64,4096]{1,0:T(8,128)(2,1)S(1)}, bf16[64,4096]{1,0:T(8,128)(2,1)S(1)}, u32[]{:S(2)}, u32[]{:S(2)}) collective-permute-start(bf16[64,4096]{1,0:T(8,128)(2,1)S(1)} %get-tuple-element.54), channel_id=1, source_target_pairs={{0,8},{8,0},{16,24},{24,16},{1,9},{9,1},{17,25},{25,17},{2,10},{10... | collective-permute-start | bytes 1572872 | tf_op jit(solution)/shard_map/ppermute | solution.py:183
  194.0 2.1 collective-permute-start.37
  196.2 14.2 %collective-permute-start.18 = (bf16[64,4096]{1,0:T(8,128)(2,1)S(1)}, bf16[64,4096]{1,0:T(8,128)(2,1)S(1)}, u32[]{:S(2)}, u32[]{:S(2)}) collective-permute-start(bf16[64,4096]{1,0:T(8,128)(2,1)S(1)} %add_convert_fusion.6), channel_id=1, source_target_pairs={{0,16},{8,24},{16,0},{24,8},{1,17},{9,25},{17,1},{25,9},{2,18},{10... | collective-permute-start | bytes 1572872 | tf_op jit(solution)/shard_map/ppermute | solution.py:186
  196.8 30.3 %collective-permute-start.36 = (bf16[64,4096]{1,0:T(8,128)(2,1)S(1)}, bf16[64,4096]{1,0:T(8,128)(2,1)S(1)}, u32[]{:S(2)}, u32[]{:S(2)}) collective-permute-start(bf16[64,4096]{1,0:T(8,128)(2,1)S(1)} %get-tuple-element.60), channel_id=1, source_target_pairs={{0,8},{8,0},{16,24},{24,16},{1,9},{9,1},{17,25},{25,17},{2,10},{10... | collective-permute-start | bytes 1572872 | tf_op jit(solution)/shard_map/ppermute | solution.py:183
  210.4 14.8 %collective-permute-start.28 = (bf16[64,4096]{1,0:T(8,128)(2,1)S(1)}, bf16[64,4096]{1,0:T(8,128)(2,1)S(1)}, u32[]{:S(2)}, u32[]{:S(2)}) collective-permute-start(bf16[64,4096]{1,0:T(8,128)(2,1)S(1)} %add_convert_fusion.4), channel_id=1, source_target_pairs={{0,16},{8,24},{16,0},{24,8},{1,17},{9,25},{17,1},{25,9},{2,18},{10... | collective-permute-start | bytes 1572872 | tf_op jit(solution)/shard_map/ppermute | solution.py:186
  211.1 23.9 %collective-permute-start.38 = (bf16[64,4096]{1,0:T(8,128)(2,1)S(1)}, bf16[64,4096]{1,0:T(8,128)(2,1)S(1)}, u32[]{:S(2)}, u32[]{:S(2)}) collective-permute-start(bf16[64,4096]{1,0:T(8,128)(2,1)S(1)} %add_convert_fusion.2), channel_id=1, source_target_pairs={{0,16},{8,24},{16,0},{24,8},{1,17},{9,25},{17,1},{25,9},{2,18},{10... | collective-permute-start | bytes 1572872 | tf_op jit(solution)/shard_map/ppermute | solution.py:186
  225.2 16.6 %collective-permute-start.19 = (bf16[64,4096]{1,0:T(8,128)(2,1)S(1)}, bf16[64,4096]{1,0:T(8,128)(2,1)S(1)}, u32[]{:S(2)}, u32[]{:S(2)}) collective-permute-start(bf16[64,4096]{1,0:T(8,128)(2,1)S(1)} %add_convert_fusion.5), channel_id=1, source_target_pairs={{0,6},{2,0},{4,2},{6,4},{1,7},{3,1},{5,3},{7,5},{8,14},{10,8},{12,... | collective-permute-start | bytes 1572872 | tf_op jit(solution)/shard_map/ppermute | solution.py:191
  227.2 30.2 %collective-permute-start.29 = (bf16[64,4096]{1,0:T(8,128)(2,1)S(1)}, bf16[64,4096]{1,0:T(8,128)(2,1)S(1)}, u32[]{:S(2)}, u32[]{:S(2)}) collective-permute-start(bf16[64,4096]{1,0:T(8,128)(2,1)S(1)} %add_convert_fusion.3), channel_id=1, source_target_pairs={{0,2},{2,4},{4,6},{6,0},{1,3},{3,5},{5,7},{7,1},{8,10},{10,12},{12... | collective-permute-start | bytes 1572872 | tf_op jit(solution)/shard_map/ppermute | solution.py:191
  235.2 39.5 %collective-permute-start.39 = (bf16[64,4096]{1,0:T(8,128)(2,1)S(1)}, bf16[64,4096]{1,0:T(8,128)(2,1)S(1)}, u32[]{:S(2)}, u32[]{:S(2)}) collective-permute-start(bf16[64,4096]{1,0:T(8,128)(2,1)S(1)} %add_convert_fusion.1), channel_id=1, source_target_pairs={{0,4},{2,6},{4,0},{6,2},{1,5},{3,7},{5,1},{7,3},{8,12},{10,14},{12... | collective-permute-start | bytes 1572872 | tf_op jit(solution)/shard_map/ppermute | solution.py:191
  (1 other events, 0.8 us)
